TPU v7x, 512 devices: a whole 4x8x8 slice. The times are simulated.
512 devices in a mesh: seq: 64 (over z_hi, y, core), head: 8 (over z_lo, x).
Axes of the slice: x: 4, y: 8, z: 8 (z_hi: 4, z_lo: 2; z = z_hi * 2 + z_lo), core: 2. Of those that a mesh axis runs over, the one named last changes fastest.
Arguments:
- query_feats: bfloat16 [32768, 4096], P('seq', 'head'), may hold values from -16 to 16
- key_feats: bfloat16 [32768, 1024], P('seq', 'head'), may hold values from -7 to 7
- value_feats: bfloat16 [32768, 1024], P('seq', 'head'), may hold values from -6 to 6
- span_class: int32 [32], replicated, may hold values from 1 to 16, as said below
- ramp_width: int32 [32], replicated, may hold values from 32 to 128
- doc_lengths: int32 [16], replicated, may hold values from 1 to 16384, 32768 in all
- out_proj: bfloat16 [4096, 4096], P('seq', 'head'), may hold values from -0.5 to 0.5
Outputs:
- mixed: bfloat16 [32768, 4096], P(('seq', 'head'))
Inputs may be any that keep to these rules, and one draw needn't show every extreme that they name: `span_class`: some head has a span of 16 tiles.
All inputs are finite; a program needn't handle non-finite values.
Results may differ from a plain program's by a relative error of at most 0.014.
Values may be sent and summed in bfloat16 or wider, within the bound.
A program may use at most 64 MiB of HBM per device.

v0:
```python
from functools import partial
import math
import jax
import jax.numpy as jnp
from jax import lax
from jax.sharding import PartitionSpec as P

HD = 128
TILE = 128
BACK = 4
very_low = -1e30


def shifted(block, axis, distance):
    devices = range(lax.axis_size(axis))
    route = [(i - distance, i) for i in devices if i - distance in devices]
    return lax.ppermute(block, axis, route)


def attend(running, key_pair, key_start, context):
    queries, query_pos, doc_start, span_end, ramp_float = context
    top_score, denominator, numerator = running
    tok_rows, kv_count, ratio, head_dim = queries.shape
    key_block = key_pair[0].reshape(tok_rows, kv_count, head_dim)
    value_block = key_pair[1].reshape(tok_rows, kv_count, head_dim)
    scores = jnp.einsum(
        "qgrd,kgd->qgrk", queries, key_block, preferred_element_type=jnp.float32
    ) * (1.0 / math.sqrt(head_dim))
    key_pos = key_start + jnp.arange(tok_rows, dtype=jnp.int32)
    distance = query_pos[:, None] - key_pos[None, :]
    visible = (distance >= 0) & (key_pos[None, :] >= doc_start[:, None])
    weights = jnp.clip(
        (span_end[None, :, :, None] - distance[:, None, None, :].astype(jnp.float32))
        / ramp_float[None, :, :, None],
        0.0,
        1.0,
    )
    weights = jnp.where(visible[:, None, None, :], weights, 0.0)
    limited = jnp.where(weights > 0.0, scores, very_low)
    new_top = jnp.maximum(top_score, jnp.max(limited, axis=3))
    rescale = jnp.exp(top_score - new_top)
    prob_terms = weights * jnp.exp(limited - new_top[:, :, :, None])
    denominator = denominator * rescale + jnp.sum(prob_terms, axis=3)
    numerator = numerator * rescale[:, :, :, None] + jnp.einsum(
        "qgrk,kgd->qgrd",
        prob_terms.astype(jnp.bfloat16),
        value_block,
        preferred_element_type=jnp.float32,
    )
    return (new_top, denominator, numerator)


def unchanged(running):
    return running


def on_device(query_feats, key_feats, value_feats, span_class, ramp_width, doc_lengths, out_proj):
    tok_rows = query_feats.shape[0]
    feat_width = query_feats.shape[1]
    head_count = feat_width // HD
    kv_count = key_feats.shape[1] // HD
    ratio = head_count // kv_count
    seq_index = lax.axis_index("seq")
    head_index = lax.axis_index("head")
    query_pos = seq_index * tok_rows + jnp.arange(tok_rows, dtype=jnp.int32)
    starts = jnp.cumsum(doc_lengths) - doc_lengths
    doc_start = jnp.max(
        jnp.where(starts[None, :] <= query_pos[:, None], starts[None, :], 0), axis=1
    )
    local_span = lax.dynamic_slice_in_dim(span_class, head_index * head_count, head_count)
    local_ramp = lax.dynamic_slice_in_dim(ramp_width, head_index * head_count, head_count)
    span_end = (local_span * TILE).astype(jnp.float32).reshape(kv_count, ratio)
    ramp_float = local_ramp.astype(jnp.float32).reshape(kv_count, ratio)
    context = (
        query_feats.reshape(tok_rows, kv_count, ratio, HD),
        query_pos,
        doc_start,
        span_end,
        ramp_float,
    )
    running = (
        jnp.full((tok_rows, kv_count, ratio), very_low, jnp.float32),
        jnp.zeros((tok_rows, kv_count, ratio), jnp.float32),
        jnp.zeros((tok_rows, kv_count, ratio, HD), jnp.float32),
    )
    own_pair = jnp.stack([key_feats, value_feats])
    running = attend(running, own_pair, seq_index * tok_rows, context)
    reach_most = jnp.max(span_end)
    moving = own_pair
    for offset in range(1, BACK + 1):
        moving = shifted(own_pair, "seq", offset)
        needed = reach_most > float((offset - 1) * tok_rows + 1)
        visit_block = partial(
            attend, key_pair=moving, key_start=(seq_index - offset) * tok_rows, context=context
        )
        running = lax.cond(needed, visit_block, unchanged, running)
    top_score, denominator, numerator = running
    attended = (
        (numerator / denominator[:, :, :, None]).astype(jnp.bfloat16).reshape(tok_rows, feat_width)
    )
    partials = lax.dot_general(
        attended,
        lax.all_gather(out_proj, "seq", axis=0, tiled=True),
        (((1,), (1,)), ((), ())),
        preferred_element_type=jnp.float32,
    )
    mixed_out = lax.psum_scatter(
        partials.astype(jnp.bfloat16), "head", scatter_dimension=0, tiled=True
    )
    return mixed_out


def solution(mesh):
    in_specs = (
        P("seq", "head"),
        P("seq", "head"),
        P("seq", "head"),
        P(),
        P(),
        P(),
        P("seq", "head"),
    )
    out_specs = P(("seq", "head"), None)
    return jax.shard_map(
        on_device, mesh=mesh, in_specs=in_specs, out_specs=out_specs, check_vma=False
    )
```

profile of v0, /device:TPU:1, one launch (start us, length us, event | category | flops | bytes accessed | tf_op | source)
XLA Modules:
  0.0 195.9 jit_solution(2180915210068702400)
XLA Ops:
  6.5 0.7 all-gather.2.cloned.1.call-update
  7.3 1.0 pad_maximum_fusion
  8.3 4.6 %collective-permute-start = (bf16[2,512,128]{2,1,0:T(8,128)(2,1)S(1)}, bf16[2,512,128]{2,1,0:T(8,128)(2,1)S(1)}, u32[]{:S(2)}, u32[]{:S(2)}) collective-permute-start(bf16[2,512,128]{2,1,0:T(8,128)(2,1)S(1)} %pad_maximum_fusion), channel_id=1, source_target_pairs={{0,8},{8,16},{16,24},{24,32},{32,40},{40,48},{48,56},{56,64},{64,7... | collective-permute-start | bytes 786440 | tf_op jit(solution)/shard_map/ppermute | solution.py:17
  12.9 3.2 %collective-permute-start.1 = (bf16[2,512,128]{2,1,0:T(8,128)(2,1)S(1)}, bf16[2,512,128]{2,1,0:T(8,128)(2,1)S(1)}, u32[]{:S(2)}, u32[]{:S(2)}) collective-permute-start(bf16[2,512,128]{2,1,0:T(8,128)(2,1)S(1)} %pad_maximum_fusion), channel_id=1, source_target_pairs={{0,16},{8,24},{16,32},{24,40},{32,48},{40,56},{48,64},{56,72},{64,... | collective-permute-start | bytes 786440 | tf_op jit(solution)/shard_map/ppermute | solution.py:17
  16.1 3.2 %collective-permute-start.2 = (bf16[2,512,128]{2,1,0:T(8,128)(2,1)S(1)}, bf16[2,512,128]{2,1,0:T(8,128)(2,1)S(1)}, u32[]{:S(2)}, u32[]{:S(2)}) collective-permute-start(bf16[2,512,128]{2,1,0:T(8,128)(2,1)S(1)} %pad_maximum_fusion), channel_id=1, source_target_pairs={{0,24},{8,32},{16,40},{24,48},{32,56},{40,64},{48,72},{56,80},{64,... | collective-permute-start | bytes 786440 | tf_op jit(solution)/shard_map/ppermute | solution.py:17
  19.3 4.5 %collective-permute-start.3 = (bf16[2,512,128]{2,1,0:T(8,128)(2,1)S(1)}, bf16[2,512,128]{2,1,0:T(8,128)(2,1)S(1)}, u32[]{:S(2)}, u32[]{:S(2)}) collective-permute-start(bf16[2,512,128]{2,1,0:T(8,128)(2,1)S(1)} %pad_maximum_fusion), channel_id=1, source_target_pairs={{0,32},{8,40},{16,48},{24,56},{32,64},{40,72},{48,80},{56,88},{64,... | collective-permute-start | bytes 786440 | tf_op jit(solution)/shard_map/ppermute | solution.py:17
  23.9 0.7 copy.32
  24.8 0.7 sub.333
  25.4 1.3 fusion.118
  26.8 0.7 dynamic-slice_convert_fusion
  27.6 0.3 fusion.107
  28.1 2.7 %fusion.93 = (f32[512,4]{0,1:T(4,128)S(1)}, f32[512,512,4]{1,0,2:T(8,128)S(1)}) fusion(f32[4]{0:T(128)S(1)} %dynamic-slice_convert_fusion, f32[512,512]{0,1:T(8,128)S(1)} %subtract_convert_fusion.4, f32[4]{0:T(128)S(1)} %get-tuple-element.311, pred[512,512]{0,1:T(8,128)(4,1)S(1)} %fusion.107, bf16[512,128]{1,0:T(8,128)(2,1)} %param.16, ...), kind=kOutput, calls=%fused_computation.117 | convolution fusion | flops 276822016 | bytes 6168608 | tf_op jit(solution)/shard_map/qgrd,kgd->qgrk/dot_general | solution.py:26
  30.8 2.2 %fusion.104 = f32[512,1,4,128]{3,0,2,1:T(8,128)S(1)} fusion(f32[512,4]{0,1:T(4,128)S(1)} %get-tuple-element.324, f32[512,512,4]{1,0,2:T(8,128)S(1)} %get-tuple-element.326, f32[4]{0:T(128)S(1)} %dynamic-slice_convert_fusion, f32[512,512]{0,1:T(8,128)S(1)} %subtract_convert_fusion.4, f32[4]{0:T(128)S(1)} %get-tuple-element.311, ...), kind=kOutput, calls=%fused_computation.126 | convolution fusion | flops 279183360 | bytes 6701088 | tf_op jit(solution)/shard_map/qgrk,kgd->qgrd/dot_general | solution.py:44
  33.1 1.9 fusion.97
  35.0 0.2 copy.35
  37.8 6.4 %conditional.4 = ((f32[512,1,4]{0,2,1:T(4,128)S(1)}, f32[512,1,4]{0,2,1:T(4,128)S(1)}, f32[512,1,4,128]{3,0,2,1:T(8,128)S(1)})) conditional(s32[]{:T(128)} %convert_element_type.87, (f32[512,1,4]{0,2,1:T(4,128)S(1)}, f32[512,1,4]{0,2,1:T(4,128)S(1)}, f32[512,1,4,128]{3,0,2,1:T(8,128)S(1)}) %tuple.37, (s32[512]{0:T(512)S(1)}, s32[]{:T(128)}, ...), branch_computations={%region_5.6_spmd, %region_6.9_spmd} | conditional | flops 568334848 | bytes 20854852 | solution.py:96
  37.8 0.1 subtract_convert_fusion
  38.0 0.3 fusion.11
  38.3 1.6 fusion
  39.9 1.9 fusion.4
  41.8 2.4 %fusion.8 = f32[512,1,4,128]{3,0,2,1:T(8,128)S(1)} fusion(f32[512,4]{0,1:T(4,128)S(1)} %bitcast.307, f32[512,512,4]{1,0,2:T(8,128)S(1)} %get-tuple-element.317, f32[4]{0:T(128)S(1)} %get-tuple-element.164, f32[512,512]{0,1:T(8,128)S(1)} %subtract_convert_fusion, f32[4]{0:T(128)S(1)} %get-tuple-element.163, pred[512,512]{0,1:T(8,128)(4,1)S(1)} %fusion.11, ...), kind=kOutput, calls=%fused_computation.11 | convolution fusion | flops 279445504 | bytes 7750656 | tf_op jit(solution)/shard_map/cond/branch_1_fun/qgrk,kgd->qgrd/dot_general | solution.py:44
  44.2 6.6 %conditional.5 = ((f32[512,1,4]{0,2,1:T(4,128)S(1)}, f32[512,1,4]{0,2,1:T(4,128)S(1)}, f32[512,1,4,128]{3,0,2,1:T(8,128)S(1)})) conditional(s32[]{:T(128)} %convert_element_type.86, (f32[512,1,4]{0,2,1:T(4,128)S(1)}, f32[512,1,4]{0,2,1:T(4,128)S(1)}, f32[512,1,4,128]{3,0,2,1:T(8,128)S(1)}) %get-tuple-element.349, (s32[512]{0:T(512)S(1)}, ...), branch_computations={%region_9.10_spmd, %region_10.13_spmd} | conditional | flops 568334848 | bytes 20854852 | solution.py:96
  44.4 0.1 subtract_convert_fusion.1
  44.6 0.3 fusion.34
  44.9 1.6 fusion.23
  46.5 1.9 fusion.27
  48.4 2.4 %fusion.31 = f32[512,1,4,128]{3,0,2,1:T(8,128)S(1)} fusion(f32[512,4]{0,1:T(4,128)S(1)} %bitcast.309, f32[512,512,4]{1,0,2:T(8,128)S(1)} %get-tuple-element.319, f32[4]{0:T(128)S(1)} %get-tuple-element.174, f32[512,512]{0,1:T(8,128)S(1)} %subtract_convert_fusion.1, f32[4]{0:T(128)S(1)} %get-tuple-element.173, pred[512,512]{0,1:T(8,128)(4,1)S(1)} %fusion.34, ...), kind=kOutput, calls=%fused_computation.39 | convolution fusion | flops 279445504 | bytes 7750656 | tf_op jit(solution)/shard_map/cond/branch_1_fun/qgrk,kgd->qgrd/dot_general | solution.py:44
  50.9 0.6 conditional.7
  50.9 0.3 copy.46
  51.6 77.0 %all-gather.2.cloned.1.call-done = bf16[4096,512]{1,0:T(8,128)(2,1)} async-done(((bf16[64,512]{1,0:T(8,128)(2,1)}), bf16[4096,512]{1,0:T(8,128)(2,1)}) %all-gather.2.cloned.1.call-update) | async-done | bytes 4194320 | tf_op jit(solution)/shard_map/all_gather | solution.py:103
  128.6 6.6 %convolution_convert_fusion = bf16[512,4096]{1,0:T(8,128)(2,1)} fusion(bf16[512,512]{0,1:T(8,128)(2,1)S(1)} %bitcast.300, bf16[4096,512]{1,0:T(8,128)(2,1)} %all-gather.2.cloned.1.call-done), kind=kOutput, calls=%fused_computation.113 | convolution fusion | flops 2149580800 | bytes 8912896 | tf_op jit(solution)/shard_map/dot_general | solution.py:101
  135.2 53.9 %reduce-scatter.2.cloned.1.call-done = bf16[64,4096]{1,0:T(8,128)(2,1)} async-done(((bf16[512,4096]{1,0:T(8,128)(2,1)}), bf16[64,4096]{1,0:T(8,128)(2,1)}) %reduce-scatter.2.cloned.1.call-update) | async-done | bytes 524304 | tf_op jit(solution)/shard_map/reduce_scatter | solution.py:107
  (28 shorter events, 0.7 us)
Async XLA Ops:
  6.5 122.1 %all-gather.2.cloned.1.call-start = ((), (), s32[]{:S(2)}) async-start(), calls=%async_computation.1 | async-start | bytes 4259840 | tf_op jit(solution)/shard_map/all_gather | solution.py:103
  7.3 181.8 %reduce-scatter.2.cloned.1.call-start = ((), (), s32[]{:S(2)}) async-start(), calls=%async_computation.2 | async-start | bytes 4718592 | tf_op jit(solution)/shard_map/reduce_scatter | solution.py:107
  8.3 29.5 %collective-permute-start = (bf16[2,512,128]{2,1,0:T(8,128)(2,1)S(1)}, bf16[2,512,128]{2,1,0:T(8,128)(2,1)S(1)}, u32[]{:S(2)}, u32[]{:S(2)}) collective-permute-start(bf16[2,512,128]{2,1,0:T(8,128)(2,1)S(1)} %pad_maximum_fusion), channel_id=1, source_target_pairs={{0,8},{8,16},{16,24},{24,32},{32,40},{40,48},{48,56},{56,64},{64,7... | collective-permute-start | bytes 786440 | tf_op jit(solution)/shard_map/ppermute | solution.py:17
  12.9 31.3 %collective-permute-start.1 = (bf16[2,512,128]{2,1,0:T(8,128)(2,1)S(1)}, bf16[2,512,128]{2,1,0:T(8,128)(2,1)S(1)}, u32[]{:S(2)}, u32[]{:S(2)}) collective-permute-start(bf16[2,512,128]{2,1,0:T(8,128)(2,1)S(1)} %pad_maximum_fusion), channel_id=1, source_target_pairs={{0,16},{8,24},{16,32},{24,40},{32,48},{40,56},{48,64},{56,72},{64,... | collective-permute-start | bytes 786440 | tf_op jit(solution)/shard_map/ppermute | solution.py:17
  16.1 34.7 %collective-permute-start.2 = (bf16[2,512,128]{2,1,0:T(8,128)(2,1)S(1)}, bf16[2,512,128]{2,1,0:T(8,128)(2,1)S(1)}, u32[]{:S(2)}, u32[]{:S(2)}) collective-permute-start(bf16[2,512,128]{2,1,0:T(8,128)(2,1)S(1)} %pad_maximum_fusion), channel_id=1, source_target_pairs={{0,24},{8,32},{16,40},{24,48},{32,56},{40,64},{48,72},{56,80},{64,... | collective-permute-start | bytes 786440 | tf_op jit(solution)/shard_map/ppermute | solution.py:17
  19.3 31.5 %collective-permute-start.3 = (bf16[2,512,128]{2,1,0:T(8,128)(2,1)S(1)}, bf16[2,512,128]{2,1,0:T(8,128)(2,1)S(1)}, u32[]{:S(2)}, u32[]{:S(2)}) collective-permute-start(bf16[2,512,128]{2,1,0:T(8,128)(2,1)S(1)} %pad_maximum_fusion), channel_id=1, source_target_pairs={{0,32},{8,40},{16,48},{24,56},{32,64},{40,72},{48,80},{56,88},{64,... | collective-permute-start | bytes 786440 | tf_op jit(solution)/shard_map/ppermute | solution.py:17
  28.1 2.8 %copy-start.1 = (bf16[512,128]{1,0:T(8,128)(2,1)S(1)}, bf16[512,128]{1,0:T(8,128)(2,1)}, u32[]{:S(2)}) copy-start(bf16[512,128]{1,0:T(8,128)(2,1)} %param.17) | copy-start | bytes 393220
  33.1 1.9 copy-start
Sparse Core Ops, SparseCore 0:
  10.7 117.8 all-gather.1
  135.3 53.6 reduce-scatter.1
where the time goes:
time: 196 us
  waiting for transfers between devices  132 us (67%)
  matrix products  19.5 us (10%)
  between operations  16.2 us (8%)
  starting transfers between devices  15.6 us (8%)
  other arithmetic  11.2 us (6%)
    all_gather x1, waiting for transfers between devices, on_device(): lax.all_gather(out_proj, 'seq', axis=0, tiled=True)  77 us
    reduce_scatter x1, waiting for transfers between devices, on_device(): lax.psum_scatter(partials.astype(jnp.bfloat16), 'head', scatter_dimension...  53.9 us
    ppermute x4, starting transfers between devices, shifted(): return lax.ppermute(block, axis, route)  15.6 us
    dot_general x3, matrix products, attend(): jnp.einsum('qgrk,kgd->qgrd', prob_terms.astype(jnp.bfloat16), value_block...  6.95 us
    dot_general x1, matrix products, on_device(): lax.dot_general(attended, lax.all_gather(out_proj, 'seq', axis=0, tiled=T...  6.56 us
    dot_general x3, matrix products, attend(): jnp.einsum('qgrd,kgd->qgrk', queries, key_block, preferred_element_type=j...  5.96 us
    reduce_sum x3, other arithmetic, attend(): denominator = denominator * rescale + jnp.sum(prob_terms, axis=3)  5.65 us
  transfers between devices with their start and end apart: 6, of which 2 were waited for; matrix products, arithmetic and copies ran while one was open for 13% of the time, Pallas kernels for 0%

commit v1 on v0

--- a/solution.py
+++ b/solution.py
@@ -100,7 +100,9 @@
     )
     partials = lax.dot_general(
         attended,
-        lax.all_gather(out_proj, "seq", axis=0, tiled=True),
+        jnp.concatenate(
+            lax.all_to_all(jnp.stack([out_proj] * lax.axis_size("seq")), "seq", 0, 0), axis=0
+        ),
         (((1,), (1,)), ((), ())),
         preferred_element_type=jnp.float32,
     )

time: 196 us -> 264 us (1.35)
  waiting for transfers between devices: 132 us -> 180 us
  starting transfers between devices: 15.6 us -> 32.2 us
  other arithmetic: 11.2 us -> 8.23 us
  local copies, waits for them, and re-layouts: 1.3 us -> 3.97 us
    ppermute x4, waiting for transfers between devices: 0.01 us -> 87.1 us  [shifted(): return lax.ppermute(block, axis, route)]
    all_gather x1 -> x0, waiting for transfers between devices: 77 us -> none  [on_device(): lax.all_gather(out_proj, 'seq', axis=0, tiled=True)]
    reduce_scatter x1, waiting for transfers between devices: 53.9 us -> 93.2 us  [on_device(): lax.psum_scatter(partials.astype(jnp.bfloat16), 'head', scatter_dimension...]
    all_to_all x0 -> x1, starting transfers between devices: none -> 18 us  [on_device(): lax.all_to_all(jnp.stack([out_proj] * lax.axis_size('seq')), 'seq', 0, 0)]
    another operation x1 -> x2, local copies, waits for them, and re-layouts: 0.73 us -> 3.4 us  [the longest x1 3.31 us: on_device(): jnp.stack([out_proj] * lax.axis_size('seq'))]
  transfers between devices with their start and end apart: 6 -> 6, of which waited for: 2 -> 2; matrix products, arithmetic and copies ran while one was open for 13% -> 9% of each run, Pallas kernels for 0% -> 0%
where the time goes in v1:
time: 264 us
  waiting for transfers between devices  180 us (68%)
  starting transfers between devices  32.2 us (12%)
  matrix products  22 us (8%)
  between operations  16.2 us (6%)
  other arithmetic  8.23 us (3%)
  local copies, waits for them, and re-layouts  3.97 us (2%)
    reduce_scatter x1, waiting for transfers between devices, on_device(): lax.psum_scatter(partials.astype(jnp.bfloat16), 'head', scatter_dimension...  93.2 us
    ppermute x4, waiting for transfers between devices, shifted(): return lax.ppermute(block, axis, route)  87.1 us
    all_to_all x1, starting transfers between devices, on_device(): lax.all_to_all(jnp.stack([out_proj] * lax.axis_size('seq')), 'seq', 0, 0)  18 us
    ppermute x4, starting transfers between devices, shifted(): return lax.ppermute(block, axis, route)  14.2 us
    dot_general x3, matrix products, attend(): jnp.einsum('qgrk,kgd->qgrd', prob_terms.astype(jnp.bfloat16), value_block...  8.77 us
    dot_general x3, matrix products, attend(): jnp.einsum('qgrd,kgd->qgrk', queries, key_block, preferred_element_type=j...  6.63 us
    dot_general x1, matrix products, on_device(): lax.dot_general(attended, jnp.concatenate(lax.all_to_all(jnp.stack([out_p...  6.56 us
    reduce_sum x3, other arithmetic, attend(): denominator = denominator * rescale + jnp.sum(prob_terms, axis=3)  5.65 us
  transfers between devices with their start and end apart: 6, of which 2 were waited for; matrix products, arithmetic and copies ran while one was open for 9% of the time, Pallas kernels for 0%

profile of v1, /device:TPU:1, one launch (start us, length us, event | category | flops | bytes accessed | tf_op | source)
XLA Modules:
  0.0 263.5 jit_solution(3817531715873493998)
XLA Ops:
  6.5 3.3 %stack.11 = bf16[64,64,512]{2,1,0:T(8,128)(2,1)} broadcast(bf16[64,512]{1,0:T(8,128)(2,1)} %param.21), dimensions={1,2} | broadcast | bytes 4259840 | tf_op jit(solution)/shard_map/stack | solution.py:104
  9.9 18.0 %all-to-all-start = ((bf16[64,64,512]{2,1,0:T(8,128)(2,1)}), bf16[64,64,512]{2,1,0:T(8,128)(2,1)}, u32[]{:S(2)}, u32[]{:S(2)}) async-start(bf16[64,64,512]{2,1,0:T(8,128)(2,1)} %stack.11), calls=%async_computation | async-start | bytes 8388608 | tf_op jit(solution)/shard_map/all_to_all | solution.py:104
  28.0 3.5 %collective-permute-start = (bf16[2,512,128]{2,1,0:T(8,128)(2,1)S(1)}, bf16[2,512,128]{2,1,0:T(8,128)(2,1)}, u32[]{:S(2)}, u32[]{:S(2)}) collective-permute-start(bf16[2,512,128]{2,1,0:T(8,128)(2,1)S(1)} %pad_maximum_fusion), channel_id=1, source_target_pairs={{0,8},{8,16},{16,24},{24,32},{32,40},{40,48},{48,56},{56,64},{64,7... | collective-permute-start | bytes 786440 | tf_op jit(solution)/shard_map/ppermute | solution.py:17
  31.5 3.8 %collective-permute-start.1 = (bf16[2,512,128]{2,1,0:T(8,128)(2,1)S(1)}, bf16[2,512,128]{2,1,0:T(8,128)(2,1)}, u32[]{:S(2)}, u32[]{:S(2)}) collective-permute-start(bf16[2,512,128]{2,1,0:T(8,128)(2,1)S(1)} %pad_maximum_fusion), channel_id=1, source_target_pairs={{0,16},{8,24},{16,32},{24,40},{32,48},{40,56},{48,64},{56,72},{64,... | collective-permute-start | bytes 786440 | tf_op jit(solution)/shard_map/ppermute | solution.py:17
  35.3 2.5 collective-permute-start.2
  37.9 4.3 %collective-permute-start.3 = (bf16[2,512,128]{2,1,0:T(8,128)(2,1)S(1)}, bf16[2,512,128]{2,1,0:T(8,128)(2,1)S(1)}, u32[]{:S(2)}, u32[]{:S(2)}) collective-permute-start(bf16[2,512,128]{2,1,0:T(8,128)(2,1)S(1)} %pad_maximum_fusion), channel_id=1, source_target_pairs={{0,32},{8,40},{16,48},{24,56},{32,64},{40,72},{48,80},{56,88},{64,... | collective-permute-start | bytes 786440 | tf_op jit(solution)/shard_map/ppermute | solution.py:17
  42.4 0.7 fusion.118
  43.3 0.3 fusion.107
  43.6 0.1 subtract_convert_fusion.4
  43.8 1.6 fusion.93
  45.4 2.2 fusion.104
  47.6 1.9 fusion.97
  49.5 0.2 copy.35
  52.3 87.1 %collective-permute-done = bf16[2,512,128]{2,1,0:T(8,128)(2,1)} collective-permute-done((bf16[2,512,128]{2,1,0:T(8,128)(2,1)S(1)}, bf16[2,512,128]{2,1,0:T(8,128)(2,1)}, u32[]{:S(2)}, u32[]{:S(2)}) %collective-permute-start) | collective-permute-done | bytes 262176 | tf_op jit(solution)/shard_map/ppermute | solution.py:17
  139.4 8.2 %conditional.4 = ((f32[512,1,4]{0,2,1:T(4,128)S(1)}, f32[512,1,4]{0,2,1:T(4,128)S(1)}, f32[512,1,4,128]{3,0,2,1:T(8,128)S(1)})) conditional(s32[]{:T(128)} %convert_element_type.87, (f32[512,1,4]{0,2,1:T(4,128)S(1)}, f32[512,1,4]{0,2,1:T(4,128)S(1)}, f32[512,1,4,128]{3,0,2,1:T(8,128)S(1)}) %tuple.37, (s32[512]{0:T(512)S(1)}, s32[]{:T(128)}, ...), branch_computations={%region_5.6_spmd, %region_6.9_spmd} | conditional | flops 568334848 | bytes 20852868 | solution.py:96
  139.4 0.1 subtract_convert_fusion
  139.6 0.3 fusion.11
  139.9 2.5 fusion
  142.4 1.9 fusion.4
  144.4 3.3 %fusion.8 = f32[512,1,4,128]{3,0,2,1:T(8,128)S(1)} fusion(f32[512,4]{0,1:T(4,128)S(1)} %bitcast.308, f32[512,512,4]{1,0,2:T(8,128)S(1)} %get-tuple-element.317, f32[4]{0:T(128)S(1)} %get-tuple-element.164, f32[512,512]{0,1:T(8,128)S(1)} %subtract_convert_fusion, f32[4]{0:T(128)S(1)} %get-tuple-element.163, pred[512,512]{0,1:T(8,128)(4,1)S(1)} %fusion.11, ...), kind=kOutput, calls=%fused_computation.11 | convolution fusion | flops 279445504 | bytes 7749664 | tf_op jit(solution)/shard_map/cond/branch_1_fun/qgrk,kgd->qgrd/dot_general | solution.py:44
  147.7 8.2 %conditional.5 = ((f32[512,1,4]{0,2,1:T(4,128)S(1)}, f32[512,1,4]{0,2,1:T(4,128)S(1)}, f32[512,1,4,128]{3,0,2,1:T(8,128)S(1)})) conditional(s32[]{:T(128)} %convert_element_type.86, (f32[512,1,4]{0,2,1:T(4,128)S(1)}, f32[512,1,4]{0,2,1:T(4,128)S(1)}, f32[512,1,4,128]{3,0,2,1:T(8,128)S(1)}) %get-tuple-element.349, (s32[512]{0:T(512)S(1)}, ...), branch_computations={%region_9.10_spmd, %region_10.13_spmd} | conditional | flops 568334848 | bytes 20852868 | solution.py:96
  147.7 0.1 subtract_convert_fusion.1
  147.8 0.3 fusion.34
  148.2 2.5 fusion.23
  150.7 1.9 fusion.27
  152.6 3.3 %fusion.31 = f32[512,1,4,128]{3,0,2,1:T(8,128)S(1)} fusion(f32[512,4]{0,1:T(4,128)S(1)} %bitcast.310, f32[512,512,4]{1,0,2:T(8,128)S(1)} %get-tuple-element.319, f32[4]{0:T(128)S(1)} %get-tuple-element.174, f32[512,512]{0,1:T(8,128)S(1)} %subtract_convert_fusion.1, f32[4]{0:T(128)S(1)} %get-tuple-element.173, pred[512,512]{0,1:T(8,128)(4,1)S(1)} %fusion.34, ...), kind=kOutput, calls=%fused_computation.39 | convolution fusion | flops 279445504 | bytes 7749664 | tf_op jit(solution)/shard_map/cond/branch_1_fun/qgrk,kgd->qgrd/dot_general | solution.py:44
  155.9 0.2 conditional.6
  156.2 0.6 conditional.7
  156.2 0.3 copy.46
  156.8 0.1 divide_convert_fusion
  156.9 6.6 %convolution_convert_fusion = bf16[512,4096]{1,0:T(8,128)(2,1)} fusion(bf16[512,512]{0,1:T(8,128)(2,1)S(1)} %bitcast.301, bf16[4096,512]{1,0:T(8,128)(2,1)} %bitcast.76), kind=kOutput, calls=%fused_computation.113 | convolution fusion | flops 2149580800 | bytes 8912896 | tf_op jit(solution)/shard_map/dot_general | solution.py:101
  163.5 93.2 %reduce-scatter.2.cloned.1.call-done = bf16[64,4096]{1,0:T(8,128)(2,1)} async-done(((bf16[512,4096]{1,0:T(8,128)(2,1)}), bf16[64,4096]{1,0:T(8,128)(2,1)}) %reduce-scatter.2.cloned.1.call-update) | async-done | bytes 524304 | tf_op jit(solution)/shard_map/reduce_scatter | solution.py:109
  (36 shorter events, 0.6 us)
Async XLA Ops:
  9.8 18.1 %copy-start.1 = (bf16[512,128]{1,0:T(8,128)(2,1)S(1)}, bf16[512,128]{1,0:T(8,128)(2,1)}, u32[]{:S(2)}) copy-start(bf16[512,128]{1,0:T(8,128)(2,1)} %param.16) | copy-start | bytes 393220
  9.9 18.1 %copy-start.2 = (bf16[512,128]{1,0:T(8,128)(2,1)S(1)}, bf16[512,128]{1,0:T(8,128)(2,1)}, u32[]{:S(2)}) copy-start(bf16[512,128]{1,0:T(8,128)(2,1)} %param.17) | copy-start | bytes 393220
  9.9 32.3 %copy-start.3 = (s32[16]{0:T(128)S(1)}, s32[16]{0:T(128)}, u32[]{:S(2)}) copy-start(s32[16]{0:T(128)} %param.20) | copy-start | bytes 196
  9.9 32.6 %copy-start.4 = (s32[32]{0:T(128)S(1)}, s32[32]{0:T(128)}, u32[]{:S(2)}) copy-start(s32[32]{0:T(128)} %param.18) | copy-start | bytes 388
  9.9 33.3 %copy-start.5 = (s32[32]{0:T(128)S(1)}, s32[32]{0:T(128)}, u32[]{:S(2)}) copy-start(s32[32]{0:T(128)} %param.19) | copy-start | bytes 388
  9.9 33.9 %copy-start = (bf16[512,512]{1,0:T(8,128)(2,1)S(1)}, bf16[512,512]{1,0:T(8,128)(2,1)}, u32[]{:S(2)}) copy-start(bf16[512,512]{1,0:T(8,128)(2,1)} %param.15) | copy-start | bytes 1572868
  9.9 147.0 %all-to-all-start = ((bf16[64,64,512]{2,1,0:T(8,128)(2,1)}), bf16[64,64,512]{2,1,0:T(8,128)(2,1)}, u32[]{:S(2)}, u32[]{:S(2)}) async-start(bf16[64,64,512]{2,1,0:T(8,128)(2,1)} %stack.11), calls=%async_computation | async-start | bytes 8388608 | tf_op jit(solution)/shard_map/all_to_all | solution.py:104
  27.9 228.8 %reduce-scatter.2.cloned.1.call-start = ((), (), s32[]{:S(2)}) async-start(), calls=%async_computation.2 | async-start | bytes 4718592 | tf_op jit(solution)/shard_map/reduce_scatter | solution.py:109
  28.0 111.5 %collective-permute-start = (bf16[2,512,128]{2,1,0:T(8,128)(2,1)S(1)}, bf16[2,512,128]{2,1,0:T(8,128)(2,1)}, u32[]{:S(2)}, u32[]{:S(2)}) collective-permute-start(bf16[2,512,128]{2,1,0:T(8,128)(2,1)S(1)} %pad_maximum_fusion), channel_id=1, source_target_pairs={{0,8},{8,16},{16,24},{24,32},{32,40},{40,48},{48,56},{56,64},{64,7... | collective-permute-start | bytes 786440 | tf_op jit(solution)/shard_map/ppermute | solution.py:17
  31.5 116.2 %collective-permute-start.1 = (bf16[2,512,128]{2,1,0:T(8,128)(2,1)S(1)}, bf16[2,512,128]{2,1,0:T(8,128)(2,1)}, u32[]{:S(2)}, u32[]{:S(2)}) collective-permute-start(bf16[2,512,128]{2,1,0:T(8,128)(2,1)S(1)} %pad_maximum_fusion), channel_id=1, source_target_pairs={{0,16},{8,24},{16,32},{24,40},{32,48},{40,56},{48,64},{56,72},{64,... | collective-permute-start | bytes 786440 | tf_op jit(solution)/shard_map/ppermute | solution.py:17
  35.3 120.6 %collective-permute-start.2 = (bf16[2,512,128]{2,1,0:T(8,128)(2,1)S(1)}, bf16[2,512,128]{2,1,0:T(8,128)(2,1)S(1)}, u32[]{:S(2)}, u32[]{:S(2)}) collective-permute-start(bf16[2,512,128]{2,1,0:T(8,128)(2,1)S(1)} %pad_maximum_fusion), channel_id=1, source_target_pairs={{0,24},{8,32},{16,40},{24,48},{32,56},{40,64},{48,72},{56,80},{64,... | collective-permute-start | bytes 786440 | tf_op jit(solution)/shard_map/ppermute | solution.py:17
  37.9 118.3 %collective-permute-start.3 = (bf16[2,512,128]{2,1,0:T(8,128)(2,1)S(1)}, bf16[2,512,128]{2,1,0:T(8,128)(2,1)S(1)}, u32[]{:S(2)}, u32[]{:S(2)}) collective-permute-start(bf16[2,512,128]{2,1,0:T(8,128)(2,1)S(1)} %pad_maximum_fusion), channel_id=1, source_target_pairs={{0,32},{8,40},{16,48},{24,56},{32,64},{40,72},{48,80},{56,88},{64,... | collective-permute-start | bytes 786440 | tf_op jit(solution)/shard_map/ppermute | solution.py:17
Sparse Core Ops, SparseCore 0:
  163.6 93.0 reduce-scatter.1
